TPU v7x, 32 devices: a whole 2x2x4 slice. The times are simulated.
32 devices in a mesh: store: 4 (over y, core), tensor: 8 (over z, x).
Axes of the slice: x: 2, y: 2, z: 4, core: 2. Of those that a mesh axis runs over, the one named last changes fastest.
Arguments:
- decoder_rows: bfloat16 [2048, 4096], P(('store', 'tensor')), may hold values from -45 to 45
- q_weight: bfloat16 [4096, 4096], P(None, 'tensor'), may hold values from -0.09375 to 0.09375
- kv_weight: bfloat16 [2, 896, 4096], P(None, None, 'tensor'), may hold values from -0.1875 to 0.1875
- out_weight: bfloat16 [4096, 4096], P('tensor'), may hold values from -0.5 to 0.5
- store_tiles: bfloat16 [2048, 128, 896], P('store', 'tensor'), may hold values from -6 to 6
- neighbour_shard: int32 [32, 2], replicated, may hold values from 0 to 3, all different within a row; in each aligned block of 8 rows (0 to 7, 8 to 15, ...) at most 6 rows name the same one
- neighbour_tile: int32 [32, 2], replicated, may hold values from 0 to 511
Outputs:
- cross: bfloat16 [2048, 4096], P(('store', 'tensor'))
Inputs may be any that keep to these rules, and one draw needn't show every extreme that they name: `neighbour_shard`: each block's 2 neighbours lie in different shards; among the 8 blocks of one sequence no shard is named more than 6 times, and in some sequence one shard is named exactly 6 times.
All inputs are finite; a program needn't handle non-finite values.
Results may differ from a plain program's by a relative error of at most 0.023.
Values may be sent and summed in bfloat16 or wider, within the bound.
A program may use at most 128 MiB of HBM per device.

v0:
```python
import math

import jax
import jax.numpy as jnp
from jax import lax
from jax.sharding import PartitionSpec as P

HD = 128
BLOCK = 64
NTOK = 128
NEIGH = 2


def body(
    decoder_rows, q_weight, kv_weight, out_weight, store_tiles, neighbour_shard, neighbour_tile
):
    tensor_count = lax.axis_size("tensor")
    store_count = lax.axis_size("store")
    my_sequence = lax.axis_index("store")
    local_rows = decoder_rows.shape[0]
    seq_len = local_rows * tensor_count
    block_count = seq_len // BLOCK
    request_count = block_count * NEIGH
    capacity = 3 * request_count // (2 * store_count)
    head_cols = q_weight.shape[1]
    head_count = head_cols // HD
    q_factor = 1.0 / math.sqrt(HD)
    rows_wide = decoder_rows.astype(jnp.float32)
    normed = (
        rows_wide * lax.rsqrt(jnp.mean(rows_wide * rows_wide, axis=1, keepdims=True) + 1e-05)
    ).astype(jnp.bfloat16)
    queries = (
        jnp.dot(
            lax.all_gather(normed, "tensor", axis=0, tiled=True),
            q_weight,
            preferred_element_type=jnp.float32,
        )
        * q_factor
    ).astype(jnp.bfloat16)
    shard_table = neighbour_shard.reshape(store_count, request_count)
    tile_table = neighbour_tile.reshape(store_count, request_count)
    positions = jnp.arange(request_count, dtype=jnp.int32)
    before_mask = positions[None, :] < positions[:, None]
    same_shard = shard_table[:, :, None] == shard_table[:, None, :]
    rank_table = jnp.sum((same_shard & before_mask[None]).astype(jnp.int32), axis=2)
    served_here = shard_table == my_sequence
    slot_ids = jnp.arange(capacity, dtype=jnp.int32)
    slot_match = (
        served_here[:, :, None] & (rank_table[:, :, None] == slot_ids[None, None, :])
    ).astype(jnp.int32)
    slot_tile = jnp.sum(slot_match * tile_table[:, :, None], axis=1)
    outgoing = jnp.take(store_tiles, slot_tile.reshape(-1), axis=0)
    arrived = lax.all_to_all(outgoing, "store", split_axis=0, concat_axis=0, tiled=True)
    own_shard = lax.dynamic_index_in_dim(shard_table, my_sequence, 0, keepdims=False)
    own_rank = lax.dynamic_index_in_dim(rank_table, my_sequence, 0, keepdims=False)
    slot_index = own_shard * capacity + own_rank
    projected = jnp.einsum(
        "rne,ced->rncd",
        jnp.take(lax.all_gather(arrived, "tensor", axis=1, tiled=True), slot_index, axis=0),
        kv_weight,
        preferred_element_type=jnp.float32,
    )
    keys_values = projected.astype(jnp.bfloat16)
    keyed = keys_values.reshape(block_count, NEIGH * NTOK, 2, head_count, HD)
    query_blocks = queries.reshape(block_count, BLOCK, head_count, HD)
    scores = jnp.einsum(
        "cqhd,ckhd->chqk", query_blocks, keyed[:, :, 0], preferred_element_type=jnp.float32
    )
    expo_scores = jnp.exp(scores)
    weights = (expo_scores / jnp.sum(expo_scores, axis=3, keepdims=True)).astype(jnp.bfloat16)
    attended = jnp.einsum(
        "chqk,ckhd->cqhd", weights, keyed[:, :, 1], preferred_element_type=jnp.float32
    )
    attended = attended.astype(jnp.bfloat16).reshape(seq_len, head_cols)
    return lax.psum_scatter(
        jnp.dot(attended, out_weight, preferred_element_type=jnp.float32).astype(jnp.bfloat16),
        "tensor",
        scatter_dimension=0,
        tiled=True,
    )


def solution(mesh):
    in_specs = (
        P(("store", "tensor"), None),
        P(None, "tensor"),
        P(None, None, "tensor"),
        P("tensor", None),
        P("store", "tensor", None),
        P(),
        P(),
    )
    out_specs = P(("store", "tensor"), None)
    return jax.shard_map(body, mesh=mesh, in_specs=in_specs, out_specs=out_specs, check_vma=False)
```

profile of v0, /device:TPU:8, one launch (start us, length us, event | category | flops | bytes accessed | tf_op | source)
XLA Modules:
  0.0 319.6 jit_solution(14024514745307070107)
XLA Ops:
  6.5 1.4 fusion.20
  7.9 2.0 fusion.21
  10.0 0.0 all-gather.3.cloned.1.call-start
  10.0 0.8 copy.18
  10.8 0.1 reshape.124
  10.9 0.8 copy.19
  11.6 0.1 mul.42
  11.7 0.2 convert_reduce_fusion
  11.9 0.2 select_reduce_fusion
  12.1 0.1 copy.20
  12.2 0.1 reshape.126
  12.3 0.1 reshape.125
  12.4 5.8 %gather_fusion = bf16[24,16,896]{2,1,0:T(8,128)(2,1)S(1)} fusion(bf16[512,16,896]{2,1,0:T(8,128)(2,1)} %param.11, s32[1024]{0:T(1024)S(1)} %pad_clamp_fusion.1), kind=kCustom, calls=%fused_computation | custom fusion | bytes 1376352 | tf_op jit(solution)/shard_map/jit(_take)/gather | solution.py:52
  18.3 0.1 broadcast_select_fusion
  18.4 13.7 %all_to_all.5 = bf16[24,16,896]{2,1,0:T(8,128)(2,1)} all-to-all(bf16[24,16,896]{2,1,0:T(8,128)(2,1)S(1)} %broadcast_select_fusion), channel_id=1, replica_groups=mesh['store'=4,'tensor'=8] {'store'}, dimensions={0} | all-to-all | bytes 1376256 | tf_op jit(solution)/shard_map/all_to_all | solution.py:53
  32.2 51.8 %all-gather.5.cloned.1.call-done = bf16[512,4096]{1,0:T(8,128)(2,1)} async-done(((bf16[64,4096]{1,0:T(8,128)(2,1)}), bf16[512,4096]{1,0:T(8,128)(2,1)}) %all-gather.5.cloned.1.call-update) | async-done | bytes 4194320 | tf_op jit(solution)/shard_map/all_gather | solution.py:34
  84.0 5.8 %fusion.13 = bf16[512,512]{1,0:T(8,128)(2,1)S(1)} fusion(bf16[512,4096]{1,0:T(8,128)(2,1)} %all-gather.5.cloned.1.call-done, bf16[4096,512]{1,0:T(8,128)(2,1)} %param.8), kind=kOutput, calls=%fused_computation.19 | convolution fusion | flops 2148007936 | bytes 8912896 | tf_op jit(solution)/shard_map/dot_general | solution.py:33
  89.8 0.1 reshape.128
  89.9 83.8 %all-gather.3.cloned.1.call-done = bf16[24,128,896]{2,1,0:T(8,128)(2,1)} async-done(((bf16[24,16,896]{2,1,0:T(8,128)(2,1)}), bf16[24,128,896]{2,1,0:T(8,128)(2,1)}) %all-gather.3.cloned.1.call-update) | async-done | bytes 5505040 | tf_op jit(solution)/shard_map/all_gather | solution.py:59
  173.7 5.4 %gather_fusion.1 = bf16[16,128,896]{2,1,0:T(8,128)(2,1)} fusion(bf16[24,128,896]{2,1,0:T(8,128)(2,1)} %all-gather.3.cloned.1.call-done, s32[1024]{0:T(1024)S(1)} %pad_clamp_fusion), kind=kCustom, calls=%fused_computation.1 | custom fusion | bytes 7340096 | tf_op jit(solution)/shard_map/jit(_take)/gather | solution.py:59
  179.1 8.2 %fusion.4 = bf16[16,128,2,512]{3,1,2,0:T(8,128)(2,1)} fusion(bf16[16,128,896]{2,1,0:T(8,128)(2,1)} %gather_fusion.1, pred[16]{0:T(512)(128)(4,1)S(1)} %get-tuple-element.5, bf16[2,896,512]{2,1,0:T(8,128)(2,1)S(1)} %copy-done), kind=kOutput, calls=%fused_computation.7 | convolution fusion | flops 3762028544 | bytes 9699344 | tf_op jit(solution)/shard_map/rne,ced->rncd/dot_general | solution.py:57
  187.3 8.0 %copy.22 = bf16[16,128,2,512]{1,0,3,2:T(8,128)(2,1)} copy(bf16[16,128,2,512]{3,1,2,0:T(8,128)(2,1)} %fusion.4) | data formatting | bytes 8388608 | tf_op jit(solution)/shard_map/convert_element_type | solution.py:63
  195.3 7.1 %reshape.127 = bf16[8,256,2,4,128]{1,0,4,3,2:T(8,128)(2,1)} reshape(bf16[16,128,2,512]{1,0,3,2:T(8,128)(2,1)} %copy.22) | data formatting | bytes 8388608 | tf_op jit(solution)/shard_map/reshape | solution.py:64
  202.4 4.5 %fusion.30 = (bf16[8,256,1,4,128]{1,0,4,3,2:T(8,128)(2,1)}, bf16[8,256,1,4,128]{1,0,4,3,2:T(8,128)(2,1)}) fusion(bf16[8,256,2,4,128]{1,0,4,3,2:T(8,128)(2,1)} %reshape.127), kind=kLoop, calls=%fused_computation.48 | loop fusion | bytes 8388608 | tf_op jit(solution)/shard_map/slice | solution.py:67
  206.9 4.5 %copy.28 = bf16[8,256,1,4,128]{4,1,3,0,2:T(8,128)(2,1)} copy(bf16[8,256,1,4,128]{1,0,4,3,2:T(8,128)(2,1)} %get-tuple-element.7) | data formatting | bytes 4194304
  211.4 4.5 %copy.29 = bf16[8,256,1,4,128]{4,1,3,0,2:T(8,128)(2,1)} copy(bf16[8,256,1,4,128]{1,0,4,3,2:T(8,128)(2,1)} %get-tuple-element.8) | data formatting | bytes 4194304
  215.9 2.7 exponential_reduce_fusion
  218.6 0.6 fusion.17
  219.2 0.4 copy.26
  219.6 1.1 copy-done.3
  220.8 4.3 %convolution_convert_fusion = bf16[512,4096]{1,0:T(8,128)(2,1)} fusion(bf16[512,4096]{1,0:T(8,128)(2,1)S(1)} %copy-done.3, bf16[64,8,4,128]{3,2,1,0:T(4,128)(2,1)S(1)} %bitcast.44), kind=kOutput, calls=%fused_computation.2 | convolution fusion | flops 2149580800 | bytes 8912896 | tf_op jit(solution)/shard_map/dot_general | solution.py:76
  225.1 88.0 %reduce-scatter.2.cloned.1.call-done = bf16[64,4096]{1,0:T(8,128)(2,1)} async-done(((bf16[512,4096]{1,0:T(8,128)(2,1)}), bf16[64,4096]{1,0:T(8,128)(2,1)}) %reduce-scatter.2.cloned.1.call-update) | async-done | bytes 524304 | tf_op jit(solution)/shard_map/reduce_scatter | solution.py:75
  (21 shorter events, 0.2 us)
Async XLA Ops:
  6.5 172.6 %copy-start = (bf16[2,896,512]{2,1,0:T(8,128)(2,1)S(1)}, bf16[2,896,512]{2,1,0:T(8,128)(2,1)}, u32[]{:S(2)}) copy-start(bf16[2,896,512]{2,1,0:T(8,128)(2,1)} %param.9) | copy-start | bytes 5505028
  6.5 77.5 %all-gather.5.cloned.1.call-start = ((), (), s32[]{:S(2)}) async-start(), calls=%async_computation.3 | async-start | bytes 4718592 | tf_op jit(solution)/shard_map/all_gather | solution.py:34
  10.0 163.8 %all-gather.3.cloned.1.call-start = ((), (), s32[]{:S(2)}) async-start(), calls=%async_computation.2 | async-start | bytes 6193152 | tf_op jit(solution)/shard_map/all_gather | solution.py:59
  32.1 280.9 %reduce-scatter.2.cloned.1.call-start = ((), (), s32[]{:S(2)}) async-start(), calls=%async_computation.4 | async-start | bytes 4718592 | tf_op jit(solution)/shard_map/reduce_scatter | solution.py:75
  215.9 2.7 copy-start.2
  218.6 2.2 copy-start.3
  220.8 92.3 %copy-start.1 = (bf16[2,896,512]{2,1,0:T(8,128)(2,1)S(1)}, bf16[2,896,512]{2,1,0:T(8,128)(2,1)}, u32[]{:S(2)}) copy-start(bf16[2,896,512]{2,1,0:T(8,128)(2,1)} %param.9) | copy-start | bytes 5505028
Sparse Core Ops, SparseCore 0:
  10.1 73.8 all-gather.4
  86.2 87.4 all-gather.2
  225.2 87.8 reduce-scatter.1
where the time goes:
time: 322 us; the launch traced here: 320 us
  waiting for transfers between devices  224 us (70%)
  local copies, waits for them, and re-layouts  43.4 us (13%)
  matrix products  21.6 us (7%)
  blocking collectives  13.7 us (4%)
  between operations  13.2 us (4%)
  other arithmetic  3.98 us (1%)
    reduce_scatter x1, waiting for transfers between devices, body(): lax.psum_scatter(jnp.dot(attended, out_weight, preferred_element_type=jnp...  88 us
    all_gather x1, waiting for transfers between devices, body(): lax.all_gather(arrived, 'tensor', axis=1, tiled=True)  83.8 us
    all_gather x1, waiting for transfers between devices, body(): lax.all_gather(normed, 'tensor', axis=0, tiled=True)  51.8 us
    all_to_all x1, blocking collectives, body(): lax.all_to_all(outgoing, 'store', split_axis=0, concat_axis=0, tiled=True)  13.7 us
    unnamed x12, local copies, waits for them, and re-layouts  11.7 us
    dot_general x1, matrix products, body(): jnp.einsum('rne,ced->rncd', jnp.take(lax.all_gather(arrived, 'tensor', ax...  8.21 us
    convert_element_type x1, local copies, waits for them, and re-layouts, body(): keys_values = projected.astype(jnp.bfloat16)  7.99 us
    reshape x1, local copies, waits for them, and re-layouts, body(): keyed = keys_values.reshape(block_count, NEIGH * NTOK, 2, head_count, HD)  7.09 us
  transfers between devices with their start and end apart: 3, of which 3 were waited for; matrix products, arithmetic and copies ran while one was open for 4% of the time, Pallas kernels for 0%

commit v1 on v0

--- a/solution.py
+++ b/solution.py
@@ -1,17 +1,431 @@
+import functools
 import math
 
 import jax
 import jax.numpy as jnp
 from jax import lax
+from jax.experimental import pallas as pl
+from jax.experimental.pallas import tpu as pltpu
 from jax.sharding import PartitionSpec as P
 
 HD = 128
 BLOCK = 64
 NTOK = 128
 NEIGH = 2
-
-
-def body(
+LINE = 4
+F32 = jnp.float32
+BF16 = jnp.bfloat16
+MESH = pl.DeviceIdType.MESH
+
+
+def pick_kernel(
+    store_count, request_count, capacity, shard_ref, tile_ref, tiles_ref, out_ref, slot_ref,
+    table, count, sem,
+):
+    me = lax.axis_index("store")
+    slots = store_count * capacity
+
+    @pl.loop(0, slots)
+    def _(i):
+        table[i] = 0
+
+    for s in range(store_count):
+        count[s] = 0
+
+        def step(r, c, s=s):
+            hit = shard_ref[s * request_count + r] == me
+            table[jnp.where(hit, s * capacity + c, slots)] = tile_ref[s * request_count + r]
+            return c + hit.astype(jnp.int32)
+
+        lax.fori_loop(0, request_count, step, jnp.int32(0))
+
+    @pl.loop(0, slots)
+    def _(i):
+        pltpu.make_async_copy(tiles_ref.at[table[i]], out_ref.at[i], sem).start()
+
+    @pl.loop(0, request_count)
+    def _(r):
+        shard = shard_ref[me * request_count + r]
+        slot_ref[r] = shard * capacity + count[shard]
+        count[shard] = count[shard] + 1
+
+    pltpu.make_async_copy(tiles_ref.at[pl.ds(0, slots)], out_ref, sem).wait()
+
+
+def main_kernel(
+    store_count, capacity, requests,
+    slot_ref, dec_ref, qw_hbm, kvw_hbm, ow_hbm, outgoing, out_ref,
+    rows, neigh, arrived, qw, kvw, ow, q_buf, k_buf, v_buf, att, part, xrecv, up, down,
+    load_sem, a2a_send, a2a_recv, rows_send, rows_recv, neigh_send, neigh_recv,
+    part_send, part_recv, chain_send, up_recv, down_recv,
+):
+    store = lax.axis_index("store")
+    tensor = lax.axis_index("tensor")
+    z = lax.div(tensor, 2)
+    x = lax.rem(tensor, 2)
+    top = LINE - 1
+    partner = z * 2 + 1 - x
+    q_factor = 1.0 / math.sqrt(HD)
+    head_count = qw.shape[1] // HD
+    tile_rows = arrived.shape[1]
+
+    loads = [
+        pltpu.make_async_copy(src, dst, load_sem.at[i])
+        for i, (src, dst) in enumerate(((kvw_hbm, kvw), (qw_hbm, qw), (ow_hbm, ow)))
+    ]
+    own_slots = pl.ds(store * capacity, capacity)
+    own_tiles = pltpu.make_async_copy(
+        outgoing.at[own_slots], arrived.at[own_slots], load_sem.at[3]
+    )
+    own_tiles.start()
+    for load in loads:
+        load.start()
+
+    barrier = pltpu.get_barrier_semaphore()
+    for k in range(1, store_count):
+        peer = lax.rem(store + k, store_count)
+        pl.semaphore_signal(barrier, inc=1, device_id=(peer, tensor), device_id_type=MESH)
+    pl.semaphore_signal(barrier, inc=1, device_id=(store, partner), device_id_type=MESH)
+
+    @pl.when(z > 0)
+    def _():
+        pl.semaphore_signal(barrier, inc=1, device_id=(store, tensor - 2), device_id_type=MESH)
+
+    @pl.when(z < top)
+    def _():
+        pl.semaphore_signal(barrier, inc=1, device_id=(store, tensor + 2), device_id_type=MESH)
+
+    inner = (z > 0) & (z < top)
+
+    @pl.when(inner)
+    def _():
+        pl.semaphore_wait(barrier, store_count + 2)
+
+    @pl.when(jnp.logical_not(inner))
+    def _():
+        pl.semaphore_wait(barrier, store_count + 1)
+
+    def tiles_copy(k):
+        peer = lax.rem(store + k, store_count)
+        return pltpu.make_async_remote_copy(
+            src_ref=outgoing.at[pl.ds(peer * capacity, capacity)],
+            dst_ref=arrived.at[own_slots],
+            send_sem=a2a_send.at[k - 1],
+            recv_sem=a2a_recv.at[k - 1],
+            device_id=(peer, tensor),
+            device_id_type=MESH,
+        )
+
+    for k in range(1, store_count):
+        tiles_copy(k).start()
+
+    def block_copy(buf, send, recv, way, j):
+        target = (tensor + 2, tensor - 2, partner)[way]
+        return pltpu.make_async_remote_copy(
+            src_ref=buf.at[j],
+            dst_ref=buf.at[j],
+            send_sem=send.at[way, j],
+            recv_sem=recv.at[j],
+            device_id=(store, target),
+            device_id_type=MESH,
+        )
+
+    row_copy = functools.partial(block_copy, rows, rows_send, rows_recv)
+    neigh_copy = functools.partial(block_copy, neigh, neigh_send, neigh_recv)
+
+    def send_own(copy):
+        @pl.when(z < top)
+        def _():
+            copy(0, tensor).start()
+
+        @pl.when(z > 0)
+        def _():
+            copy(1, tensor).start()
+
+        copy(2, tensor).start()
+
+    def forward(copy, d):
+        @pl.when(z - d >= 0)
+        def _():
+            j = tensor - 2 * d
+            copy(0, j).wait_recv()
+
+            @pl.when(z < top)
+            def _():
+                copy(0, j).start()
+
+            copy(2, j).start()
+
+        @pl.when(z + d <= top)
+        def _():
+            j = tensor + 2 * d
+            copy(1, j).wait_recv()
+
+            @pl.when(z > 0)
+            def _():
+                copy(1, j).start()
+
+            copy(2, j).start()
+
+    @pl.loop(0, dec_ref.shape[0] // 16)
+    def _(i):
+        at = pl.ds(pl.multiple_of(i * 16, 16), 16)
+        wide = dec_ref[at, :].astype(F32)
+        scale = lax.rsqrt(jnp.mean(wide * wide, axis=1, keepdims=True) + 1e-05)
+        rows[tensor, at, :] = (wide * scale).astype(BF16)
+
+    send_own(row_copy)
+
+    own_tiles.wait()
+    for k in range(1, store_count):
+        tiles_copy(k).wait_recv()
+
+    @pl.loop(0, requests)
+    def _(r):
+        picked = arrived[slot_ref[r]]
+        neigh[tensor, pl.ds(pl.multiple_of(r * tile_rows, tile_rows), tile_rows), :] = picked
+
+    send_own(neigh_copy)
+
+    def project(j):
+        source = neigh[j]
+        for a, dst in ((0, k_buf), (1, v_buf)):
+            got = jnp.dot(source, kvw[a], preferred_element_type=F32).astype(BF16)
+            dst[j] = got.reshape(dst.shape[1:])
+
+    loads[0].wait()
+    project(tensor)
+
+    @pl.loop(1, LINE)
+    def _(d):
+        forward(row_copy, d)
+        forward(neigh_copy, d)
+
+        @pl.when(z - d >= 0)
+        def _():
+            project(tensor - 2 * d)
+
+        @pl.when(z + d <= top)
+        def _():
+            project(tensor + 2 * d)
+
+    for p in range(LINE):
+        row_copy(2, p * 2 + 1 - x).wait_recv()
+    loads[1].wait()
+
+    @pl.loop(0, qw.shape[1] // 256)
+    def _(c):
+        at = pl.ds(pl.multiple_of(c * 256, 256), 256)
+        all_rows = rows[...].reshape(-1, rows.shape[2])
+        got = jnp.dot(all_rows, qw[:, at], preferred_element_type=F32)
+        q_buf[:, :, at] = (got * q_factor).astype(BF16).reshape(q_buf.shape[0], BLOCK, 256)
+
+    half = lax.div(z, 2)
+    near = z + half * (3 - 2 * z)
+
+    def place(k):
+        o = (3, 2 - 2 * near, 1 + near, near)[k]
+        return o + half * (3 - 2 * o)
+
+    for k in reversed(range(LINE)):
+        j = place(k) * 2 + 1 - x
+        neigh_copy(2, j).wait_recv()
+        project(j)
+    loads[2].wait()
+
+    def part_copy(p):
+        return pltpu.make_async_remote_copy(
+            src_ref=part.at[p, 1 - x],
+            dst_ref=xrecv.at[p],
+            send_sem=part_send.at[p],
+            recv_sem=part_recv.at[p],
+            device_id=(store, partner),
+            device_id_type=MESH,
+        )
+
+    def chain_copy(way, p):
+        return pltpu.make_async_remote_copy(
+            src_ref=part.at[p, x],
+            dst_ref=(up, down)[way].at[p],
+            send_sem=chain_send.at[p],
+            recv_sem=(up_recv, down_recv)[way].at[p],
+            device_id=(store, (tensor + 2, tensor - 2)[way]),
+            device_id_type=MESH,
+        )
+
+    def attend(p):
+        @pl.loop(0, 2)
+        def _(i):
+            b = p * 2 + i
+            for h in range(head_count):
+                cols = slice(h * HD, (h + 1) * HD)
+                keys = k_buf[:, b, :, cols].reshape(-1, HD)
+                values = v_buf[:, b, :, cols].reshape(-1, HD)
+                scores = lax.dot_general(
+                    q_buf[b, :, cols], keys, (((1,), (1,)), ((), ())),
+                    preferred_element_type=F32,
+                )
+                expo = jnp.exp(scores)
+                weights = (expo / jnp.sum(expo, axis=1, keepdims=True)).astype(BF16)
+                got = jnp.dot(weights, values, preferred_element_type=F32)
+                att[i, :, cols] = got.astype(BF16)
+
+        @pl.loop(0, ow.shape[1] // 512)
+        def _(c):
+            at = pl.ds(pl.multiple_of(c * 512, 512), 512)
+            both = att[...].reshape(-1, att.shape[2])
+            got = jnp.dot(both, ow[:, at], preferred_element_type=F32).astype(BF16)
+            part[p, :, :, at] = got.reshape(2, BLOCK, 512)
+
+        part_copy(p).start()
+
+    def add(p, *terms):
+        @pl.loop(0, BLOCK // 16)
+        def _(i):
+            at = pl.ds(pl.multiple_of(i * 16, 16), 16)
+            total = part[p, x, at, :].astype(F32)
+            for term in terms:
+                total = total + term[p, at, :].astype(F32)
+            part[p, x, at, :] = total.astype(BF16)
+
+    def pass_on(p):
+        part_copy(p).wait_recv()
+        add(p, xrecv)
+
+        @pl.when(p > z)
+        def _():
+            @pl.when(z > 0)
+            def _():
+                chain_copy(0, p).wait_recv()
+                add(p, up)
+
+            chain_copy(0, p).start()
+
+        @pl.when(p < z)
+        def _():
+            @pl.when(z < top)
+            def _():
+                chain_copy(1, p).wait_recv()
+                add(p, down)
+
+            chain_copy(1, p).start()
+
+    attend(place(0))
+    attend(place(1))
+    pass_on(place(0))
+    attend(place(2))
+    pass_on(place(1))
+    attend(place(3))
+    pass_on(place(2))
+    part_copy(z).wait_recv()
+    add(z, xrecv)
+
+    @pl.when(z > 0)
+    def _():
+        chain_copy(0, z).wait_recv()
+        add(z, up)
+
+    @pl.when(z < top)
+    def _():
+        chain_copy(1, z).wait_recv()
+        add(z, down)
+
+    out_ref[...] = part[z, x]
+
+    for k in range(1, store_count):
+        tiles_copy(k).wait_send()
+    for copy in (row_copy, neigh_copy):
+        for p in range(LINE):
+            j = p * 2 + x
+
+            @pl.when((p <= z) & (z < top))
+            def _():
+                copy(0, j).wait_send()
+
+            @pl.when((p >= z) & (z > 0))
+            def _():
+                copy(1, j).wait_send()
+
+            copy(2, j).wait_send()
+    for p in range(LINE):
+        part_copy(p).wait_send()
+
+        @pl.when(z != p)
+        def _():
+            chain_copy(0, p).wait_send()
+
+
+def kernel_body(
+    decoder_rows, q_weight, kv_weight, out_weight, store_tiles, neighbour_shard, neighbour_tile
+):
+    tensor_count = lax.axis_size("tensor")
+    store_count = lax.axis_size("store")
+    local_rows, width = decoder_rows.shape
+    blocks = tensor_count * local_rows // BLOCK
+    requests = blocks * NEIGH
+    capacity = 3 * requests // (2 * store_count)
+    slots = store_count * capacity
+    tile_rows, enc = store_tiles.shape[1:]
+    head_cols = q_weight.shape[1]
+    hbm = pl.BlockSpec(memory_space=pl.ANY)
+    smem = pl.BlockSpec(memory_space=pltpu.SMEM)
+    vmem = pl.BlockSpec(memory_space=pltpu.VMEM)
+    outgoing, slot_index = pl.pallas_call(
+        functools.partial(pick_kernel, store_count, requests, capacity),
+        out_shape=(
+            jax.ShapeDtypeStruct((slots, tile_rows, enc), BF16),
+            jax.ShapeDtypeStruct((requests,), jnp.int32),
+        ),
+        in_specs=[smem, smem, hbm],
+        out_specs=(hbm, smem),
+        scratch_shapes=[
+            pltpu.SMEM((slots + 1,), jnp.int32),
+            pltpu.SMEM((store_count,), jnp.int32),
+            pltpu.SemaphoreType.DMA,
+        ],
+    )(neighbour_shard.reshape(-1), neighbour_tile.reshape(-1), store_tiles)
+    dma = pltpu.SemaphoreType.DMA
+    block_keys = NEIGH * tile_rows
+    return pl.pallas_call(
+        functools.partial(main_kernel, store_count, capacity, requests),
+        out_shape=jax.ShapeDtypeStruct((local_rows, width), BF16),
+        in_specs=[smem, vmem, hbm, hbm, hbm, hbm],
+        out_specs=vmem,
+        scratch_shapes=[
+            pltpu.VMEM((tensor_count, local_rows, width), BF16),
+            pltpu.VMEM((tensor_count, requests * tile_rows, enc), BF16),
+            pltpu.VMEM((slots, tile_rows, enc), BF16),
+            pltpu.VMEM(q_weight.shape, BF16),
+            pltpu.VMEM(kv_weight.shape, BF16),
+            pltpu.VMEM(out_weight.shape, BF16),
+            pltpu.VMEM((blocks, BLOCK, head_cols), BF16),
+            pltpu.VMEM((tensor_count, blocks, block_keys, head_cols), BF16),
+            pltpu.VMEM((tensor_count, blocks, block_keys, head_cols), BF16),
+            pltpu.VMEM((2, BLOCK, head_cols), BF16),
+            pltpu.VMEM((LINE, 2, BLOCK, width), BF16),
+            pltpu.VMEM((LINE, BLOCK, width), BF16),
+            pltpu.VMEM((LINE, BLOCK, width), BF16),
+            pltpu.VMEM((LINE, BLOCK, width), BF16),
+            dma((4,)),
+            dma((store_count - 1,)),
+            dma((store_count - 1,)),
+            dma((3, tensor_count)),
+            dma((tensor_count,)),
+            dma((3, tensor_count)),
+            dma((tensor_count,)),
+            dma((LINE,)),
+            dma((LINE,)),
+            dma((LINE,)),
+            dma((LINE,)),
+            dma((LINE,)),
+        ],
+        compiler_params=pltpu.CompilerParams(
+            collective_id=0, has_side_effects=True, vmem_limit_bytes=56 * 2**20
+        ),
+    )(slot_index, decoder_rows, q_weight, kv_weight, out_weight, outgoing)
+
+
+def plain_body(
     decoder_rows, q_weight, kv_weight, out_weight, store_tiles, neighbour_shard, neighbour_tile
 ):
     tensor_count = lax.axis_size("tensor")
@@ -54,9 +468,10 @@
     own_shard = lax.dynamic_index_in_dim(shard_table, my_sequence, 0, keepdims=False)
     own_rank = lax.dynamic_index_in_dim(rank_table, my_sequence, 0, keepdims=False)
     slot_index = own_shard * capacity + own_rank
+    picked = jnp.take(arrived, slot_index, axis=0)
     projected = jnp.einsum(
         "rne,ced->rncd",
-        jnp.take(lax.all_gather(arrived, "tensor", axis=1, tiled=True), slot_index, axis=0),
+        lax.all_gather(picked, "tensor", axis=1, tiled=True),
         kv_weight,
         preferred_element_type=jnp.float32,
     )
@@ -78,6 +493,15 @@
         scatter_dimension=0,
         tiled=True,
     )
+
+
+def body(*args):
+    fits = (
+        lax.axis_size("tensor") == 2 * LINE
+        and args[0].shape[0] == BLOCK
+        and args[4].shape[1] % 16 == 0
+    )
+    return (kernel_body if fits else plain_body)(*args)
 
 
 def solution(mesh):

time: 322 us -> 178 us (0.55)
  waiting for transfers between devices: 224 us -> 0 us
  Pallas kernels: 0 us -> 173 us
  local copies, waits for them, and re-layouts: 43.4 us -> 4.63 us
  matrix products: 21.6 us -> 0 us
  blocking collectives: 13.7 us -> 0 us
  between operations: 13.2 us -> 0.02 us
  other arithmetic: 3.98 us -> 0 us
    pallas_call x0 -> x2, Pallas kernels: none -> 173 us  [the longest x1 149 us: kernel_body(): pl.pallas_call(functools.partial(main_kernel, store_count, capacity, requ...]
    all_gather x2 -> x0, waiting for transfers between devices: 136 us -> none  [the longest x1 83.8 us: body(): lax.all_gather(arrived, 'tensor', axis=1, tiled=True)]
    reduce_scatter x1 -> x0, waiting for transfers between devices: 88 us -> none  [body(): lax.psum_scatter(jnp.dot(attended, out_weight, preferred_element_type=jnp...]
    dot_general x5 -> x0, matrix products: 21.6 us -> none  [the longest x1 8.21 us: body(): jnp.einsum('rne,ced->rncd', jnp.take(lax.all_gather(arrived, 'tensor', ax...]
    all_to_all x1 -> x0, blocking collectives: 13.7 us -> none  [body(): lax.all_to_all(outgoing, 'store', split_axis=0, concat_axis=0, tiled=True)]
    gather x2 -> x0, local copies, waits for them, and re-layouts: 11.2 us -> none  [the longest x1 5.84 us: body(): outgoing = jnp.take(store_tiles, slot_tile.reshape(-1), axis=0)]
    convert_element_type x2 -> x0, local copies, waits for them, and re-layouts: 8.4 us -> none  [the longest x1 7.99 us: body(): keys_values = projected.astype(jnp.bfloat16)]
    unnamed x12 -> x3, local copies, waits for them, and re-layouts: 11.7 us -> 3.39 us
  transfers between devices with their start and end apart: 3 -> 0, of which waited for: 3 -> 0; matrix products, arithmetic and copies ran while one was open for 4% -> 0% of each run, Pallas kernels for 0% -> 0%
where the time goes in v1:
time: 178 us
  Pallas kernels  173 us (97%)
  local copies, waits for them, and re-layouts  4.63 us (3%)
    pallas_call x1, Pallas kernels, kernel_body(): pl.pallas_call(functools.partial(main_kernel, store_count, capacity, requ...  149 us
    pallas_call x1, Pallas kernels, kernel_body(): pl.pallas_call(functools.partial(pick_kernel, store_count, requests, capa...  23.8 us

profile of v1, /device:TPU:8, one launch (start us, length us, event | category | flops | bytes accessed | tf_op | source)
XLA Modules:
  0.0 177.7 jit_solution(13828057980257400452)
XLA Ops:
  0.0 0.8 copy.10
  0.8 0.6 reshape.6.shard_ref
  1.4 0.8 copy.11
  2.1 0.6 reshape.7.tile_ref
  2.8 23.8 %shard_map.73 = (bf16[24,16,896]{2,1,0:T(8,128)(2,1)}, s32[16]{0:T(128)}) custom-call(s32[64]{0:T(128)} %reshape.6.shard_ref, s32[64]{0:T(128)} %reshape.7.tile_ref, bf16[512,16,896]{2,1,0:T(8,128)(2,1)} %tiles_ref.1), custom_call_target="tpu_custom_call" | custom-call | tf_op jit(solution)/shard_map/pallas_call | solution.py:373
  26.5 149.3 %shard_map.74 = bf16[64,4096]{1,0:T(8,128)(2,1)} custom-call(s32[16]{0:T(128)} %get-tuple-element.7.slot_ref, bf16[64,4096]{1,0:T(8,128)(2,1)} %dec_ref.1, bf16[4096,512]{1,0:T(8,128)(2,1)} %qw_hbm.1, bf16[2,896,512]{2,1,0:T(8,128)(2,1)} %kvw_hbm.1, bf16[512,4096]{1,0:T(8,128)(2,1)} %ow_hbm.1, bf16[24,16,896]{2,1,0:T(8,128)(2,1)} %get-tuple-element.8.outgoing), custom_call_target="tpu_custom_call" | custom-call | tf_op jit(solution)/shard_map/pallas_call | solution.py:389
  175.8 1.9 %copy.13 = bf16[64,4096]{1,0:T(8,128)(2,1)} copy(bf16[64,4096]{1,0:T(8,128)(2,1)} %shard_map.74) | data formatting | bytes 1048576

commit v2 on v1

--- a/solution.py
+++ b/solution.py
@@ -18,44 +18,10 @@
 MESH = pl.DeviceIdType.MESH
 
 
-def pick_kernel(
-    store_count, request_count, capacity, shard_ref, tile_ref, tiles_ref, out_ref, slot_ref,
-    table, count, sem,
-):
-    me = lax.axis_index("store")
-    slots = store_count * capacity
-
-    @pl.loop(0, slots)
-    def _(i):
-        table[i] = 0
-
-    for s in range(store_count):
-        count[s] = 0
-
-        def step(r, c, s=s):
-            hit = shard_ref[s * request_count + r] == me
-            table[jnp.where(hit, s * capacity + c, slots)] = tile_ref[s * request_count + r]
-            return c + hit.astype(jnp.int32)
-
-        lax.fori_loop(0, request_count, step, jnp.int32(0))
-
-    @pl.loop(0, slots)
-    def _(i):
-        pltpu.make_async_copy(tiles_ref.at[table[i]], out_ref.at[i], sem).start()
-
-    @pl.loop(0, request_count)
-    def _(r):
-        shard = shard_ref[me * request_count + r]
-        slot_ref[r] = shard * capacity + count[shard]
-        count[shard] = count[shard] + 1
-
-    pltpu.make_async_copy(tiles_ref.at[pl.ds(0, slots)], out_ref, sem).wait()
-
-
 def main_kernel(
     store_count, capacity, requests,
-    slot_ref, dec_ref, qw_hbm, kvw_hbm, ow_hbm, outgoing, out_ref,
-    rows, neigh, arrived, qw, kvw, ow, q_buf, k_buf, v_buf, att, part, xrecv, up, down,
+    shard_ref, tile_ref, dec_ref, qw_hbm, kvw_hbm, ow_hbm, tiles_hbm, out_ref,
+    rows, neigh, table, tiles, outgoing, arrived, qw, kvw, ow, q_buf, k_buf, v_buf, att, part, xrecv, up, down,
     load_sem, a2a_send, a2a_recv, rows_send, rows_recv, neigh_send, neigh_recv,
     part_send, part_recv, chain_send, up_recv, down_recv,
 ):
@@ -71,13 +37,11 @@
 
     loads = [
         pltpu.make_async_copy(src, dst, load_sem.at[i])
-        for i, (src, dst) in enumerate(((kvw_hbm, kvw), (qw_hbm, qw), (ow_hbm, ow)))
+        for i, (src, dst) in enumerate(
+            ((tiles_hbm, tiles), (kvw_hbm, kvw), (qw_hbm, qw), (ow_hbm, ow))
+        )
     ]
     own_slots = pl.ds(store * capacity, capacity)
-    own_tiles = pltpu.make_async_copy(
-        outgoing.at[own_slots], arrived.at[own_slots], load_sem.at[3]
-    )
-    own_tiles.start()
     for load in loads:
         load.start()
 
@@ -94,6 +58,13 @@
     @pl.when(z < top)
     def _():
         pl.semaphore_signal(barrier, inc=1, device_id=(store, tensor + 2), device_id_type=MESH)
+
+    @pl.loop(0, dec_ref.shape[0] // 16)
+    def _(i):
+        at = pl.ds(pl.multiple_of(i * 16, 16), 16)
+        wide = dec_ref[at, :].astype(F32)
+        scale = lax.rsqrt(jnp.mean(wide * wide, axis=1, keepdims=True) + 1e-05)
+        rows[tensor, at, :] = (wide * scale).astype(BF16)
 
     inner = (z > 0) & (z < top)
 
@@ -116,9 +87,6 @@
             device_id_type=MESH,
         )
 
-    for k in range(1, store_count):
-        tiles_copy(k).start()
-
     def block_copy(buf, send, recv, way, j):
         target = (tensor + 2, tensor - 2, partner)[way]
         return pltpu.make_async_remote_copy(
@@ -167,23 +135,43 @@
 
             copy(2, j).start()
 
-    @pl.loop(0, dec_ref.shape[0] // 16)
+    send_own(row_copy)
+
+    for s in range(store_count):
+        wanted = [jnp.int32(0)] * capacity
+        seen = jnp.int32(0)
+        for r in range(requests):
+            n, b = r % NEIGH, (s * requests + r) // NEIGH
+            hit = shard_ref[n, b] == store
+            tile = tile_ref[n, b]
+            for c in range(min(r + 1, capacity)):
+                wanted[c] = jnp.where(hit & (seen == c), tile, wanted[c])
+            seen = seen + hit.astype(jnp.int32)
+        for c in range(capacity):
+            table[s * capacity + c] = wanted[c]
+
+    loads[0].wait()
+
+    @pl.loop(0, store_count * capacity)
     def _(i):
-        at = pl.ds(pl.multiple_of(i * 16, 16), 16)
-        wide = dec_ref[at, :].astype(F32)
-        scale = lax.rsqrt(jnp.mean(wide * wide, axis=1, keepdims=True) + 1e-05)
-        rows[tensor, at, :] = (wide * scale).astype(BF16)
-
-    send_own(row_copy)
-
-    own_tiles.wait()
+        outgoing[i] = tiles[table[i]]
+
+    for k in range(1, store_count):
+        tiles_copy(k).start()
+
+    for c in range(capacity):
+        arrived[store * capacity + c] = outgoing[store * capacity + c]
     for k in range(1, store_count):
         tiles_copy(k).wait_recv()
 
-    @pl.loop(0, requests)
-    def _(r):
-        picked = arrived[slot_ref[r]]
-        neigh[tensor, pl.ds(pl.multiple_of(r * tile_rows, tile_rows), tile_rows), :] = picked
+    counts = [jnp.int32(0)] * store_count
+    for r in range(requests):
+        shard = shard_ref[r % NEIGH, store * (requests // NEIGH) + r // NEIGH]
+        slot = shard * capacity
+        for k in range(store_count):
+            slot = slot + jnp.where(shard == k, counts[k], 0)
+            counts[k] = counts[k] + (shard == k).astype(jnp.int32)
+        neigh[tensor, pl.ds(r * tile_rows, tile_rows), :] = arrived[slot]
 
     send_own(neigh_copy)
 
@@ -193,7 +181,7 @@
             got = jnp.dot(source, kvw[a], preferred_element_type=F32).astype(BF16)
             dst[j] = got.reshape(dst.shape[1:])
 
-    loads[0].wait()
+    loads[1].wait()
     project(tensor)
 
     @pl.loop(1, LINE)
@@ -211,7 +199,7 @@
 
     for p in range(LINE):
         row_copy(2, p * 2 + 1 - x).wait_recv()
-    loads[1].wait()
+    loads[2].wait()
 
     @pl.loop(0, qw.shape[1] // 256)
     def _(c):
@@ -231,7 +219,7 @@
         j = place(k) * 2 + 1 - x
         neigh_copy(2, j).wait_recv()
         project(j)
-    loads[2].wait()
+    loads[3].wait()
 
     def part_copy(p):
         return pltpu.make_async_remote_copy(
@@ -370,30 +358,19 @@
     hbm = pl.BlockSpec(memory_space=pl.ANY)
     smem = pl.BlockSpec(memory_space=pltpu.SMEM)
     vmem = pl.BlockSpec(memory_space=pltpu.VMEM)
-    outgoing, slot_index = pl.pallas_call(
-        functools.partial(pick_kernel, store_count, requests, capacity),
-        out_shape=(
-            jax.ShapeDtypeStruct((slots, tile_rows, enc), BF16),
-            jax.ShapeDtypeStruct((requests,), jnp.int32),
-        ),
-        in_specs=[smem, smem, hbm],
-        out_specs=(hbm, smem),
-        scratch_shapes=[
-            pltpu.SMEM((slots + 1,), jnp.int32),
-            pltpu.SMEM((store_count,), jnp.int32),
-            pltpu.SemaphoreType.DMA,
-        ],
-    )(neighbour_shard.reshape(-1), neighbour_tile.reshape(-1), store_tiles)
     dma = pltpu.SemaphoreType.DMA
     block_keys = NEIGH * tile_rows
     return pl.pallas_call(
         functools.partial(main_kernel, store_count, capacity, requests),
         out_shape=jax.ShapeDtypeStruct((local_rows, width), BF16),
-        in_specs=[smem, vmem, hbm, hbm, hbm, hbm],
+        in_specs=[smem, smem, vmem, hbm, hbm, hbm, hbm],
         out_specs=vmem,
         scratch_shapes=[
             pltpu.VMEM((tensor_count, local_rows, width), BF16),
             pltpu.VMEM((tensor_count, requests * tile_rows, enc), BF16),
+            pltpu.SMEM((slots,), jnp.int32),
+            pltpu.VMEM(store_tiles.shape, BF16),
+            pltpu.VMEM((slots, tile_rows, enc), BF16),
             pltpu.VMEM((slots, tile_rows, enc), BF16),
             pltpu.VMEM(q_weight.shape, BF16),
             pltpu.VMEM(kv_weight.shape, BF16),
@@ -422,7 +399,10 @@
         compiler_params=pltpu.CompilerParams(
             collective_id=0, has_side_effects=True, vmem_limit_bytes=56 * 2**20
         ),
-    )(slot_index, decoder_rows, q_weight, kv_weight, out_weight, outgoing)
+    )(
+        neighbour_shard.T, neighbour_tile.T, decoder_rows, q_weight, kv_weight, out_weight,
+        store_tiles,
+    )
 
 
 def plain_body(

time: 178 us -> 153 us (0.86)
  the two profiles are of different devices: /device:TPU:8 before, /device:TPU:21 now
where the time goes in v2:
time: 153 us
  Pallas kernels  151 us (99%)
  local copies, waits for them, and re-layouts  1.87 us (1%)
    pallas_call x1, Pallas kernels, kernel_body(): pl.pallas_call(functools.partial(main_kernel, store_count, capacity, requ...  151 us

profile of v2, /device:TPU:21, one launch (start us, length us, event | category | flops | bytes accessed | tf_op | source)
XLA Modules:
  0.0 152.7 jit_solution(6553040992766195801)
XLA Ops:
  0.0 150.9 %shard_map.73 = bf16[64,4096]{1,0:T(8,128)(2,1)} custom-call(s32[2,32]{1,0:T(2,128)} %bitcast.2, s32[2,32]{1,0:T(2,128)} %bitcast.3, bf16[64,4096]{1,0:T(8,128)(2,1)} %dec_ref.1, bf16[4096,512]{1,0:T(8,128)(2,1)} %qw_hbm.1, bf16[2,896,512]{2,1,0:T(8,128)(2,1)} %kvw_hbm.1, bf16[512,4096]{1,0:T(8,128)(2,1)} %ow_hbm.1, bf16[512,16,896]{2,1,0:T(8,128)(2,1)} %tiles_hbm.1), custom_call_target="tpu_custom_call" | custom-call | tf_op jit(solution)/shard_map/pallas_call | solution.py:363
  150.9 1.9 %copy.9 = bf16[64,4096]{1,0:T(8,128)(2,1)} copy(bf16[64,4096]{1,0:T(8,128)(2,1)} %shard_map.73) | data formatting | bytes 1048576

commit v3 on v2

--- a/solution.py
+++ b/solution.py
@@ -21,9 +21,11 @@
 def main_kernel(
     store_count, capacity, requests,
     shard_ref, tile_ref, dec_ref, qw_hbm, kvw_hbm, ow_hbm, tiles_hbm, out_ref,
-    rows, neigh, table, tiles, outgoing, arrived, qw, kvw, ow, q_buf, k_buf, v_buf, att, part, xrecv, up, down,
+    rows, neigh, table, tiles, outgoing, arrived, qw, kvw, ow, q_buf, k_buf, v_buf, att,
+    part, xrecv, up, down, side_up, side_down, side_x,
     load_sem, a2a_send, a2a_recv, rows_send, rows_recv, neigh_send, neigh_recv,
     part_send, part_recv, chain_send, up_recv, down_recv,
+    edge_send, edge_recv, edge_x, side_send, side_up_recv, side_down_recv, side_x_sem,
 ):
     store = lax.axis_index("store")
     tensor = lax.axis_index("tensor")
@@ -34,6 +36,9 @@
     q_factor = 1.0 / math.sqrt(HD)
     head_count = qw.shape[1] // HD
     tile_rows = arrived.shape[1]
+    width = rows.shape[2]
+    cut = width * 11 // 16
+    side = width * 13 // 16
 
     loads = [
         pltpu.make_async_copy(src, dst, load_sem.at[i])
@@ -87,19 +92,41 @@
             device_id_type=MESH,
         )
 
-    def block_copy(buf, send, recv, way, j):
+    def block_copy(buf, columns, send, recv, way, j):
         target = (tensor + 2, tensor - 2, partner)[way]
         return pltpu.make_async_remote_copy(
-            src_ref=buf.at[j],
-            dst_ref=buf.at[j],
+            src_ref=buf.at[j, :, pl.ds(0, columns)],
+            dst_ref=buf.at[j, :, pl.ds(0, columns)],
             send_sem=send.at[way, j],
             recv_sem=recv.at[j],
             device_id=(store, target),
             device_id_type=MESH,
         )
 
-    row_copy = functools.partial(block_copy, rows, rows_send, rows_recv)
-    neigh_copy = functools.partial(block_copy, neigh, neigh_send, neigh_recv)
+    row_copy = functools.partial(block_copy, rows, cut, rows_send, rows_recv)
+    neigh_copy = functools.partial(block_copy, neigh, neigh.shape[2], neigh_send, neigh_recv)
+
+    def edge_across(j):
+        at = rows.at[j, :, pl.ds(cut, width - cut)]
+        return pltpu.make_async_remote_copy(
+            src_ref=at,
+            dst_ref=at,
+            send_sem=edge_x.at[0],
+            recv_sem=edge_x.at[1],
+            device_id=(store, partner),
+            device_id_type=MESH,
+        )
+
+    def edge_copy(way, p):
+        at = rows.at[pl.ds(p * 2, 2), :, pl.ds(cut, width - cut)]
+        return pltpu.make_async_remote_copy(
+            src_ref=at,
+            dst_ref=at,
+            send_sem=edge_send.at[way, p],
+            recv_sem=edge_recv.at[p],
+            device_id=(store, (tensor + 2, tensor - 2)[way]),
+            device_id_type=MESH,
+        )
 
     def send_own(copy):
         @pl.when(z < top)
@@ -135,6 +162,7 @@
 
             copy(2, j).start()
 
+    edge_across(tensor).start()
     send_own(row_copy)
 
     for s in range(store_count):
@@ -174,6 +202,15 @@
         neigh[tensor, pl.ds(r * tile_rows, tile_rows), :] = arrived[slot]
 
     send_own(neigh_copy)
+    edge_across(partner).wait_recv()
+
+    @pl.when(z < top)
+    def _():
+        edge_copy(0, z).start()
+
+    @pl.when(z > 0)
+    def _():
+        edge_copy(1, z).start()
 
     def project(j):
         source = neigh[j]
@@ -187,6 +224,23 @@
     @pl.loop(1, LINE)
     def _(d):
         forward(row_copy, d)
+
+        @pl.when(z - d >= 0)
+        def _():
+            edge_copy(0, z - d).wait_recv()
+
+            @pl.when(z < top)
+            def _():
+                edge_copy(0, z - d).start()
+
+        @pl.when(z + d <= top)
+        def _():
+            edge_copy(1, z + d).wait_recv()
+
+            @pl.when(z > 0)
+            def _():
+                edge_copy(1, z + d).start()
+
         forward(neigh_copy, d)
 
         @pl.when(z - d >= 0)
@@ -223,7 +277,7 @@
 
     def part_copy(p):
         return pltpu.make_async_remote_copy(
-            src_ref=part.at[p, 1 - x],
+            src_ref=part.at[p, 1 - x, :, pl.ds(0, side)],
             dst_ref=xrecv.at[p],
             send_sem=part_send.at[p],
             recv_sem=part_recv.at[p],
@@ -233,13 +287,60 @@
 
     def chain_copy(way, p):
         return pltpu.make_async_remote_copy(
-            src_ref=part.at[p, x],
+            src_ref=part.at[p, x, :, pl.ds(0, side)],
             dst_ref=(up, down)[way].at[p],
             send_sem=chain_send.at[p],
             recv_sem=(up_recv, down_recv)[way].at[p],
             device_id=(store, (tensor + 2, tensor - 2)[way]),
             device_id_type=MESH,
         )
+
+    def side_copy(way, p):
+        return pltpu.make_async_remote_copy(
+            src_ref=part.at[p, :, :, pl.ds(side, width - side)],
+            dst_ref=(side_up, side_down)[way].at[p],
+            send_sem=side_send.at[p],
+            recv_sem=(side_up_recv, side_down_recv)[way].at[p],
+            device_id=(store, (tensor + 2, tensor - 2)[way]),
+            device_id_type=MESH,
+        )
+
+    def side_across():
+        return pltpu.make_async_remote_copy(
+            src_ref=part.at[z, 1 - x, :, pl.ds(side, width - side)],
+            dst_ref=side_x,
+            send_sem=side_x_sem.at[0],
+            recv_sem=side_x_sem.at[1],
+            device_id=(store, partner),
+            device_id_type=MESH,
+        )
+
+    def add_side(p, term):
+        @pl.loop(0, 2 * BLOCK // 16)
+        def _(i):
+            c = lax.div(i, BLOCK // 16)
+            at = pl.ds(pl.multiple_of(lax.rem(i, BLOCK // 16) * 16, 16), 16)
+            total = part[p, c, at, side:].astype(F32) + term[p, c, at, :].astype(F32)
+            part[p, c, at, side:] = total.astype(BF16)
+
+    def pass_side(p):
+        @pl.when(p > z)
+        def _():
+            @pl.when(z > 0)
+            def _():
+                side_copy(0, p).wait_recv()
+                add_side(p, side_up)
+
+            side_copy(0, p).start()
+
+        @pl.when(p < z)
+        def _():
+            @pl.when(z < top)
+            def _():
+                side_copy(1, p).wait_recv()
+                add_side(p, side_down)
+
+            side_copy(1, p).start()
 
     def attend(p):
         @pl.loop(0, 2)
@@ -271,10 +372,10 @@
         @pl.loop(0, BLOCK // 16)
         def _(i):
             at = pl.ds(pl.multiple_of(i * 16, 16), 16)
-            total = part[p, x, at, :].astype(F32)
+            total = part[p, x, at, :side].astype(F32)
             for term in terms:
                 total = total + term[p, at, :].astype(F32)
-            part[p, x, at, :] = total.astype(BF16)
+            part[p, x, at, :side] = total.astype(BF16)
 
     def pass_on(p):
         part_copy(p).wait_recv()
@@ -300,11 +401,25 @@
 
     attend(place(0))
     attend(place(1))
+    pass_side(place(0))
     pass_on(place(0))
     attend(place(2))
+    pass_side(place(1))
     pass_on(place(1))
     attend(place(3))
+    pass_side(place(2))
     pass_on(place(2))
+    @pl.when(z > 0)
+    def _():
+        side_copy(0, z).wait_recv()
+        add_side(z, side_up)
+
+    @pl.when(z < top)
+    def _():
+        side_copy(1, z).wait_recv()
+        add_side(z, side_down)
+
+    side_across().start()
     part_copy(z).wait_recv()
     add(z, xrecv)
 
@@ -318,7 +433,12 @@
         chain_copy(1, z).wait_recv()
         add(z, down)
 
-    out_ref[...] = part[z, x]
+    out_ref[:, :side] = part[z, x, :, :side]
+    side_across().wait_recv()
+    last = part[z, x, :, side:].astype(F32) + side_x[...].astype(F32)
+    out_ref[:, side:] = last.astype(BF16)
+    side_across().wait_send()
+    edge_across(tensor).wait_send()
 
     for k in range(1, store_count):
         tiles_copy(k).wait_send()
@@ -341,6 +461,15 @@
         @pl.when(z != p)
         def _():
             chain_copy(0, p).wait_send()
+            side_copy(0, p).wait_send()
+
+        @pl.when((p <= z) & (z < top))
+        def _():
+            edge_copy(0, p).wait_send()
+
+        @pl.when((p >= z) & (z > 0))
+        def _():
+            edge_copy(1, p).wait_send()
 
 
 def kernel_body(
@@ -360,6 +489,7 @@
     vmem = pl.BlockSpec(memory_space=pltpu.VMEM)
     dma = pltpu.SemaphoreType.DMA
     block_keys = NEIGH * tile_rows
+    side = width * 13 // 16
     return pl.pallas_call(
         functools.partial(main_kernel, store_count, capacity, requests),
         out_shape=jax.ShapeDtypeStruct((local_rows, width), BF16),
@@ -380,9 +510,12 @@
             pltpu.VMEM((tensor_count, blocks, block_keys, head_cols), BF16),
             pltpu.VMEM((2, BLOCK, head_cols), BF16),
             pltpu.VMEM((LINE, 2, BLOCK, width), BF16),
-            pltpu.VMEM((LINE, BLOCK, width), BF16),
-            pltpu.VMEM((LINE, BLOCK, width), BF16),
-            pltpu.VMEM((LINE, BLOCK, width), BF16),
+            pltpu.VMEM((LINE, BLOCK, side), BF16),
+            pltpu.VMEM((LINE, BLOCK, side), BF16),
+            pltpu.VMEM((LINE, BLOCK, side), BF16),
+            pltpu.VMEM((LINE, 2, BLOCK, width - side), BF16),
+            pltpu.VMEM((LINE, 2, BLOCK, width - side), BF16),
+            pltpu.VMEM((BLOCK, width - side), BF16),
             dma((4,)),
             dma((store_count - 1,)),
             dma((store_count - 1,)),
@@ -395,6 +528,13 @@
             dma((LINE,)),
             dma((LINE,)),
             dma((LINE,)),
+            dma((2, LINE)),
+            dma((LINE,)),
+            dma((2,)),
+            dma((LINE,)),
+            dma((LINE,)),
+            dma((LINE,)),
+            dma((2,)),
         ],
         compiler_params=pltpu.CompilerParams(
             collective_id=0, has_side_effects=True, vmem_limit_bytes=56 * 2**20

time: 153 us -> 153 us (level)
  the two profiles are of different devices: /device:TPU:21 before, /device:TPU:8 now
where the time goes in v3:
time: 153 us
  Pallas kernels  151 us (99%)
  local copies, waits for them, and re-layouts  1.87 us (1%)
    pallas_call x1, Pallas kernels, kernel_body(): pl.pallas_call(functools.partial(main_kernel, store_count, capacity, requ...  151 us

profile of v3, /device:TPU:8, one launch (start us, length us, event | category | flops | bytes accessed | tf_op | source)
XLA Modules:
  0.0 152.8 jit_solution(2378716124021306703)
XLA Ops:
  0.0 150.9 %shard_map.73 = bf16[64,4096]{1,0:T(8,128)(2,1)} custom-call(s32[2,32]{1,0:T(2,128)} %bitcast.2, s32[2,32]{1,0:T(2,128)} %bitcast.3, bf16[64,4096]{1,0:T(8,128)(2,1)} %dec_ref.1, bf16[4096,512]{1,0:T(8,128)(2,1)} %qw_hbm.1, bf16[2,896,512]{2,1,0:T(8,128)(2,1)} %kvw_hbm.1, bf16[512,4096]{1,0:T(8,128)(2,1)} %ow_hbm.1, bf16[512,16,896]{2,1,0:T(8,128)(2,1)} %tiles_hbm.1), custom_call_target="tpu_custom_call" | custom-call | tf_op jit(solution)/shard_map/pallas_call | solution.py:493
  150.9 1.9 %copy.9 = bf16[64,4096]{1,0:T(8,128)(2,1)} copy(bf16[64,4096]{1,0:T(8,128)(2,1)} %shard_map.73) | data formatting | bytes 1048576

commit v4 on v2

--- a/solution.py
+++ b/solution.py
@@ -21,9 +21,11 @@
 def main_kernel(
     store_count, capacity, requests,
     shard_ref, tile_ref, dec_ref, qw_hbm, kvw_hbm, ow_hbm, tiles_hbm, out_ref,
-    rows, neigh, table, tiles, outgoing, arrived, qw, kvw, ow, q_buf, k_buf, v_buf, att, part, xrecv, up, down,
+    rows, neigh, table, tiles, outgoing, arrived, qw, kvw, ow, q_buf, k_buf, v_buf, att,
+    part, xrecv, up, down,
     load_sem, a2a_send, a2a_recv, rows_send, rows_recv, neigh_send, neigh_recv,
     part_send, part_recv, chain_send, up_recv, down_recv,
+    edge_send, edge_recv, edge_x,
 ):
     store = lax.axis_index("store")
     tensor = lax.axis_index("tensor")
@@ -34,6 +36,8 @@
     q_factor = 1.0 / math.sqrt(HD)
     head_count = qw.shape[1] // HD
     tile_rows = arrived.shape[1]
+    width = rows.shape[2]
+    cut = width * 11 // 16
 
     loads = [
         pltpu.make_async_copy(src, dst, load_sem.at[i])
@@ -87,19 +91,41 @@
             device_id_type=MESH,
         )
 
-    def block_copy(buf, send, recv, way, j):
+    def block_copy(buf, columns, send, recv, way, j):
         target = (tensor + 2, tensor - 2, partner)[way]
         return pltpu.make_async_remote_copy(
-            src_ref=buf.at[j],
-            dst_ref=buf.at[j],
+            src_ref=buf.at[j, :, pl.ds(0, columns)],
+            dst_ref=buf.at[j, :, pl.ds(0, columns)],
             send_sem=send.at[way, j],
             recv_sem=recv.at[j],
             device_id=(store, target),
             device_id_type=MESH,
         )
 
-    row_copy = functools.partial(block_copy, rows, rows_send, rows_recv)
-    neigh_copy = functools.partial(block_copy, neigh, neigh_send, neigh_recv)
+    row_copy = functools.partial(block_copy, rows, cut, rows_send, rows_recv)
+    neigh_copy = functools.partial(block_copy, neigh, neigh.shape[2], neigh_send, neigh_recv)
+
+    def edge_across(j):
+        at = rows.at[j, :, pl.ds(cut, width - cut)]
+        return pltpu.make_async_remote_copy(
+            src_ref=at,
+            dst_ref=at,
+            send_sem=edge_x.at[0],
+            recv_sem=edge_x.at[1],
+            device_id=(store, partner),
+            device_id_type=MESH,
+        )
+
+    def edge_copy(way, p):
+        at = rows.at[pl.ds(p * 2, 2), :, pl.ds(cut, width - cut)]
+        return pltpu.make_async_remote_copy(
+            src_ref=at,
+            dst_ref=at,
+            send_sem=edge_send.at[way, p],
+            recv_sem=edge_recv.at[p],
+            device_id=(store, (tensor + 2, tensor - 2)[way]),
+            device_id_type=MESH,
+        )
 
     def send_own(copy):
         @pl.when(z < top)
@@ -135,6 +161,7 @@
 
             copy(2, j).start()
 
+    edge_across(tensor).start()
     send_own(row_copy)
 
     for s in range(store_count):
@@ -174,6 +201,15 @@
         neigh[tensor, pl.ds(r * tile_rows, tile_rows), :] = arrived[slot]
 
     send_own(neigh_copy)
+    edge_across(partner).wait_recv()
+
+    @pl.when(z < top)
+    def _():
+        edge_copy(0, z).start()
+
+    @pl.when(z > 0)
+    def _():
+        edge_copy(1, z).start()
 
     def project(j):
         source = neigh[j]
@@ -187,6 +223,23 @@
     @pl.loop(1, LINE)
     def _(d):
         forward(row_copy, d)
+
+        @pl.when(z - d >= 0)
+        def _():
+            edge_copy(0, z - d).wait_recv()
+
+            @pl.when(z < top)
+            def _():
+                edge_copy(0, z - d).start()
+
+        @pl.when(z + d <= top)
+        def _():
+            edge_copy(1, z + d).wait_recv()
+
+            @pl.when(z > 0)
+            def _():
+                edge_copy(1, z + d).start()
+
         forward(neigh_copy, d)
 
         @pl.when(z - d >= 0)
@@ -300,10 +353,19 @@
 
     attend(place(0))
     attend(place(1))
-    pass_on(place(0))
+
+    @pl.when(jnp.logical_not(inner))
+    def _():
+        pass_on(place(0))
+
     attend(place(2))
+    attend(place(3))
+
+    @pl.when(inner)
+    def _():
+        pass_on(place(0))
+
     pass_on(place(1))
-    attend(place(3))
     pass_on(place(2))
     part_copy(z).wait_recv()
     add(z, xrecv)
@@ -319,6 +381,7 @@
         add(z, down)
 
     out_ref[...] = part[z, x]
+    edge_across(tensor).wait_send()
 
     for k in range(1, store_count):
         tiles_copy(k).wait_send()
@@ -341,6 +404,14 @@
         @pl.when(z != p)
         def _():
             chain_copy(0, p).wait_send()
+
+        @pl.when((p <= z) & (z < top))
+        def _():
+            edge_copy(0, p).wait_send()
+
+        @pl.when((p >= z) & (z > 0))
+        def _():
+            edge_copy(1, p).wait_send()
 
 
 def kernel_body(
@@ -395,6 +466,9 @@
             dma((LINE,)),
             dma((LINE,)),
             dma((LINE,)),
+            dma((2, LINE)),
+            dma((LINE,)),
+            dma((2,)),
         ],
         compiler_params=pltpu.CompilerParams(
             collective_id=0, has_side_effects=True, vmem_limit_bytes=56 * 2**20

time: 153 us -> 155 us (1.013)
  the two profiles are of different devices: /device:TPU:21 before, /device:TPU:8 now
where the time goes in v4:
time: 155 us; the launch traced here: 153 us
  Pallas kernels  151 us (97%)
  local copies, waits for them, and re-layouts  1.87 us (1%)
    pallas_call x1, Pallas kernels, kernel_body(): pl.pallas_call(functools.partial(main_kernel, store_count, capacity, requ...  151 us

profile of v4, /device:TPU:8, one launch (start us, length us, event | category | flops | bytes accessed | tf_op | source)
XLA Modules:
  0.0 153.1 jit_solution(5846549055269277037)
XLA Ops:
  0.0 151.2 %shard_map.73 = bf16[64,4096]{1,0:T(8,128)(2,1)} custom-call(s32[2,32]{1,0:T(2,128)} %bitcast.2, s32[2,32]{1,0:T(2,128)} %bitcast.3, bf16[64,4096]{1,0:T(8,128)(2,1)} %dec_ref.1, bf16[4096,512]{1,0:T(8,128)(2,1)} %qw_hbm.1, bf16[2,896,512]{2,1,0:T(8,128)(2,1)} %kvw_hbm.1, bf16[512,4096]{1,0:T(8,128)(2,1)} %ow_hbm.1, bf16[512,16,896]{2,1,0:T(8,128)(2,1)} %tiles_hbm.1), custom_call_target="tpu_custom_call" | custom-call | tf_op jit(solution)/shard_map/pallas_call | solution.py:434
  151.2 1.9 %copy.9 = bf16[64,4096]{1,0:T(8,128)(2,1)} copy(bf16[64,4096]{1,0:T(8,128)(2,1)} %shard_map.73) | data formatting | bytes 1048576

commit v5 on v3

--- a/solution.py
+++ b/solution.py
@@ -218,12 +218,11 @@
             got = jnp.dot(source, kvw[a], preferred_element_type=F32).astype(BF16)
             dst[j] = got.reshape(dst.shape[1:])
 
-    loads[1].wait()
-    project(tensor)
 
     @pl.loop(1, LINE)
     def _(d):
         forward(row_copy, d)
+        forward(neigh_copy, d)
 
         @pl.when(z - d >= 0)
         def _():
@@ -241,15 +240,11 @@
             def _():
                 edge_copy(1, z + d).start()
 
-        forward(neigh_copy, d)
-
-        @pl.when(z - d >= 0)
-        def _():
-            project(tensor - 2 * d)
-
-        @pl.when(z + d <= top)
-        def _():
-            project(tensor + 2 * d)
+    loads[1].wait()
+
+    @pl.loop(0, LINE)
+    def _(p):
+        project(p * 2 + x)
 
     for p in range(LINE):
         row_copy(2, p * 2 + 1 - x).wait_recv()
@@ -401,12 +396,26 @@
 
     attend(place(0))
     attend(place(1))
-    pass_side(place(0))
-    pass_on(place(0))
+
+    @pl.when(jnp.logical_not(inner))
+    def _():
+        pass_side(place(0))
+        pass_on(place(0))
+
     attend(place(2))
+
+    @pl.when(inner)
+    def _():
+        pass_side(place(0))
+
+    attend(place(3))
+
+    @pl.when(inner)
+    def _():
+        pass_on(place(0))
+
     pass_side(place(1))
     pass_on(place(1))
-    attend(place(3))
     pass_side(place(2))
     pass_on(place(2))
     @pl.when(z > 0)

time: 153 us -> 145 us (0.948)
  Pallas kernels: 151 us -> 141 us
    pallas_call x1, Pallas kernels: 151 us -> 141 us  [kernel_body(): pl.pallas_call(functools.partial(main_kernel, store_count, capacity, requ...]
where the time goes in v5:
time: 145 us; the launch traced here: 143 us
  Pallas kernels  141 us (97%)
  local copies, waits for them, and re-layouts  1.87 us (1%)
    pallas_call x1, Pallas kernels, kernel_body(): pl.pallas_call(functools.partial(main_kernel, store_count, capacity, requ...  141 us

profile of v5, /device:TPU:8, one launch (start us, length us, event | category | flops | bytes accessed | tf_op | source)
XLA Modules:
  0.0 143.4 jit_solution(11440498380632595975)
XLA Ops:
  0.0 141.5 %shard_map.73 = bf16[64,4096]{1,0:T(8,128)(2,1)} custom-call(s32[2,32]{1,0:T(2,128)} %bitcast.2, s32[2,32]{1,0:T(2,128)} %bitcast.3, bf16[64,4096]{1,0:T(8,128)(2,1)} %dec_ref.1, bf16[4096,512]{1,0:T(8,128)(2,1)} %qw_hbm.1, bf16[2,896,512]{2,1,0:T(8,128)(2,1)} %kvw_hbm.1, bf16[512,4096]{1,0:T(8,128)(2,1)} %ow_hbm.1, bf16[512,16,896]{2,1,0:T(8,128)(2,1)} %tiles_hbm.1), custom_call_target="tpu_custom_call" | custom-call | tf_op jit(solution)/shard_map/pallas_call | solution.py:502
  141.5 1.9 %copy.9 = bf16[64,4096]{1,0:T(8,128)(2,1)} copy(bf16[64,4096]{1,0:T(8,128)(2,1)} %shard_map.73) | data formatting | bytes 1048576
